TPU v7x, 256 devices: a whole 4x4x8 slice. The times are simulated.
256 devices in a mesh: seg: 16 (over x, y_lo, core), sub: 16 (over z, y_hi).
Axes of the slice: x: 4, y: 4 (y_hi: 2, y_lo: 2; y = y_hi * 2 + y_lo), z: 8, core: 2. Of those that a mesh axis runs over, the one named last changes fastest.
Arguments:
- edge_mid: float32 [16, 3, 4096], P('sub', None, 'seg'), may hold values from -1 to 1
- edge_dir: float32 [16, 3, 4096], P('sub', None, 'seg'), may hold values from -6 to 6
- seg_mid: float32 [3, 4096], P(None, 'seg'), may hold values from -1.5 to 1.5
- seg_vec: float32 [3, 4096], P(None, 'seg'), may hold values from -0.09375 to 0.09375
- currents: float32 [128, 4096], P(None, 'seg'), may hold values from -6 to 6
- flexibility: float32 [16, 4096, 4096], P('sub', 'seg'), as said below
- partner: int32 [6, 16], replicated, may hold values from 0 to 15, as said below
- edge_block: int32 [6, 16, 24], P(None, 'sub'), may hold values from 0 to 255, as said below
Outputs:
- multipliers: float32 [16, 6, 384, 128], P('sub', None, 'seg')
- trace: float32 [16, 4096, 128], P('sub', 'seg')
Inputs may be any that keep to these rules, and one draw needn't show every extreme that they name: For each round the subdomains are matched in pairs: partner[r, j] != j and partner[r, partner[r, j]] == j. For each subdomain j the 144 entries edge_block[:, j, :] are distinct. Each flexibility[j] is symmetric and positive definite.
All inputs are finite; a program needn't handle non-finite values.
Results may differ from a plain program's by a relative error of at most 0.0003.
Values sent between devices are 32-bit elements; how exact they have to be, the bound alone decides.
A program may use at most 64 MiB of HBM per device.

v0:
```python
import jax
import jax.numpy as jnp
from jax import lax
from jax.sharding import PartitionSpec as P

ITERS = 4


core_radius = 0.05
highest = lax.Precision.HIGHEST


def kernel_tile(edge_mid, edge_dir, seg_mid, seg_vec):
    distance = jnp.zeros((edge_mid.shape[1], seg_mid.shape[1]), jnp.float32)
    aligned = jnp.zeros((edge_mid.shape[1], seg_mid.shape[1]), jnp.float32)
    for component in range(3):
        spacing = edge_mid[component][:, None] - seg_mid[component][None, :]
        distance = distance + spacing * spacing
        aligned = aligned + edge_dir[component][:, None] * seg_vec[component][None, :]
    return aligned / jnp.sqrt(distance + core_radius * core_radius)


def contract_segments(kernel, currents):
    return lax.dot_general(
        kernel,
        currents,
        (((1,), (1,)), ((), ())),
        precision=highest,
        preferred_element_type=jnp.float32,
    )


def body(edge_mid, edge_dir, seg_mid, seg_vec, currents, flexibility, partner, edge_block):
    my_mid = edge_mid[0]
    my_dir = edge_dir[0]
    row_count = my_mid.shape[1]
    patterns = currents.shape[0]
    all_mid, all_dir = (
        lax.all_gather(my_mid, "seg", axis=1, tiled=True),
        lax.all_gather(my_dir, "seg", axis=1, tiled=True),
    )
    sources = lax.psum_scatter(
        contract_segments(kernel_tile(all_mid, all_dir, seg_mid, seg_vec), currents),
        "seg",
        scatter_dimension=0,
        tiled=True,
    )
    flex_rows = flexibility[0]

    def schur_apply(trace_in):
        return jnp.dot(
            flex_rows,
            lax.all_gather(trace_in, "seg", axis=0, tiled=True),
            precision=highest,
            preferred_element_type=jnp.float32,
        )

    me_index = lax.axis_index("sub")
    my_partner = lax.dynamic_index_in_dim(partner, me_index, 1, keepdims=False)
    upper_side = my_partner > me_index
    sign_of = jnp.where(upper_side, 1.0, -1.0).astype(jnp.float32)
    owners = jnp.where(upper_side, 1.0, 0.0).astype(jnp.float32)
    offsets_here = edge_block[:, 0, :]

    def jump_of(trace_in):
        picked = jnp.take(trace_in, offsets_here, axis=0)
        pieces = lax.all_gather(picked[None], "sub", axis=0, tiled=True)
        sources_at = jnp.arange(pieces.shape[0], dtype=jnp.int32)
        hits = my_partner[None, :] == sources_at[:, None]
        opposite = jnp.sum(jnp.where(hits[:, :, None, None], pieces, 0.0), axis=0)
        return sign_of[:, None, None] * (picked - opposite)

    def local_inner(first, second):
        return jnp.sum(owners[:, None, None] * first * second, axis=(0, 1))

    def squares(residual):
        return lax.psum(local_inner(residual, residual), ("seg", "sub"))

    base_trace = schur_apply(sources)
    right_side = jump_of(base_trace)
    multipliers = jnp.zeros_like(right_side)
    carried = jnp.zeros_like(base_trace)
    residual = right_side
    direction = right_side
    norm_now = squares(residual)
    for iteration in range(ITERS):
        image_trace = schur_apply(
            jnp.zeros((row_count, patterns), jnp.float32)
            .at[offsets_here]
            .add(sign_of[:, None, None] * direction)
        )
        image_dual = jump_of(image_trace)
        curve = lax.psum(local_inner(direction, image_dual), ("seg", "sub"))
        step_size = norm_now / curve
        multipliers = multipliers + step_size * direction
        residual = residual - step_size * image_dual
        carried = carried + step_size * image_trace
        if iteration + 1 < ITERS:
            norm_next = squares(residual)
            direction = residual + norm_next / norm_now * direction
            norm_now = norm_next
    return (multipliers[None], (base_trace - carried)[None])


def solution(mesh):
    in_specs = (
        P("sub", None, "seg"),
        P("sub", None, "seg"),
        P(None, "seg"),
        P(None, "seg"),
        P(None, "seg"),
        P("sub", "seg", None),
        P(),
        P(None, "sub", None),
    )
    out_specs = (P("sub", None, "seg", None), P("sub", "seg", None))
    return jax.shard_map(body, mesh=mesh, in_specs=in_specs, out_specs=out_specs, check_vma=False)
```

profile of v0, /device:TPU:1, one launch (start us, length us, event | category | flops | bytes accessed | tf_op | source)
XLA Modules:
  0.0 1269.4 jit_solution(4812048012368342339)
XLA Ops:
  8.8 21.4 %all-gather.1 = f32[1,3,4096]{2,0,1:T(1,128)S(1)} all-gather(f32[1,3,256]{2,0,1:T(1,128)} %param.10), channel_id=3, replica_groups=mesh['seg'=16,'sub'=16] {'seg'}, dimensions={2}, use_global_device_ids=true | all-gather | bytes 52224 | tf_op jit(solution)/shard_map/all_gather | solution.py:39
  30.2 16.6 %all-gather = f32[1,3,4096]{2,0,1:T(1,128)S(1)} all-gather(f32[1,3,256]{2,0,1:T(1,128)} %param.11), channel_id=2, replica_groups=mesh['seg'=16,'sub'=16] {'seg'}, dimensions={2}, use_global_device_ids=true | all-gather | bytes 52224 | tf_op jit(solution)/shard_map/all_gather | solution.py:40
  46.9 8.2 fusion.10
  55.1 62.9 %reduce-scatter.2.cloned.1.call-done = f32[256,128]{1,0:T(8,128)} async-done(((f32[4096,128]{1,0:T(8,128)}), f32[256,128]{1,0:T(8,128)}) %reduce-scatter.2.cloned.1.call-update) | async-done | bytes 131088 | tf_op jit(solution)/shard_map/reduce_scatter | solution.py:42
  118.3 40.6 %all-gather.18.cloned.1.call-done = f32[4096,128]{1,0:T(8,128)} async-done(((f32[256,128]{1,0:T(8,128)}), f32[4096,128]{1,0:T(8,128)}) %all-gather.18.cloned.1.call-update) | async-done | bytes 2097168 | tf_op jit(solution)/shard_map/all_gather | solution.py:53
  158.9 6.3 fusion.40
  167.0 75.5 %all-gather.28.cloned.1.call-done = f32[96,24,128]{2,1,0:T(8,128)} async-done(((f32[6,24,128]{2,1,0:T(8,128)}), f32[96,24,128]{2,1,0:T(8,128)}) %all-gather.28.cloned.1.call-update) | async-done | bytes 1179664 | tf_op jit(solution)/shard_map/all_gather | solution.py:67
  242.5 1.4 select_reduce_fusion.4
  244.0 1.7 scatter_custom_fusion
  245.8 37.5 %all-gather.20.cloned.1.call-done = f32[4096,128]{1,0:T(8,128)} async-done(((f32[256,128]{1,0:T(8,128)}), f32[4096,128]{1,0:T(8,128)}) %all-gather.20.cloned.1.call-update) | async-done | bytes 2097168 | tf_op jit(solution)/shard_map/all_gather | solution.py:53
  283.3 6.3 fusion.43
  291.1 75.8 %all-gather.30.cloned.1.call-done = f32[96,24,128]{2,1,0:T(8,128)} async-done(((f32[6,24,128]{2,1,0:T(8,128)}), f32[96,24,128]{2,1,0:T(8,128)}) %all-gather.30.cloned.1.call-update) | async-done | bytes 1179664 | tf_op jit(solution)/shard_map/all_gather | solution.py:67
  368.5 78.3 %all-reduce = (f32[128]{0:T(128)S(1)}, f32[128]{0:T(128)S(1)}) all-reduce(f32[128]{0:T(128)S(1)} %get-tuple-element.8, f32[128]{0:T(128)S(1)} %get-tuple-element.7), channel_id=1, replica_groups=mesh['seg'=16,'sub'=16] {'seg','sub'}, use_global_device_ids=true, to_apply=%region_3.5 | all-reduce | flops 256 | bytes 2048 | tf_op jit(solution)/shard_map/psum | solution.py:77
  446.9 72.5 %psum.58 = f32[128]{0:T(128)S(1)} all-reduce(f32[128]{0:T(128)S(1)} %fusion.57), channel_id=1, replica_groups=mesh['seg'=16,'sub'=16] {'seg','sub'}, use_global_device_ids=true, to_apply=%region_9.11 | all-reduce | flops 128 | bytes 1024 | tf_op jit(solution)/shard_map/psum | solution.py:77
  519.5 1.7 scatter_custom_fusion.1
  521.3 33.6 %all-gather.22.cloned.1.call-done = f32[4096,128]{1,0:T(8,128)} async-done(((f32[256,128]{1,0:T(8,128)}), f32[4096,128]{1,0:T(8,128)}) %all-gather.22.cloned.1.call-update) | async-done | bytes 2097168 | tf_op jit(solution)/shard_map/all_gather | solution.py:53
  554.8 6.3 fusion.46
  562.7 75.8 %all-gather.32.cloned.1.call-done = f32[96,24,128]{2,1,0:T(8,128)} async-done(((f32[6,24,128]{2,1,0:T(8,128)}), f32[96,24,128]{2,1,0:T(8,128)}) %all-gather.32.cloned.1.call-update) | async-done | bytes 1179664 | tf_op jit(solution)/shard_map/all_gather | solution.py:67
  638.5 1.4 select_reduce_fusion.2
  640.0 78.3 %psum.59 = f32[128]{0:T(128)S(1)} all-reduce(f32[128]{0:T(128)S(1)} %multiply_reduce_fusion.2), channel_id=1, replica_groups=mesh['seg'=16,'sub'=16] {'seg','sub'}, use_global_device_ids=true, to_apply=%region_13.15 | all-reduce | flops 128 | bytes 1024 | tf_op jit(solution)/shard_map/psum | solution.py:93
  718.5 72.3 %psum.60 = f32[128]{0:T(128)S(1)} all-reduce(f32[128]{0:T(128)S(1)} %get-tuple-element.17), channel_id=1, replica_groups=mesh['seg'=16,'sub'=16] {'seg','sub'}, use_global_device_ids=true, to_apply=%region_15.17 | all-reduce | flops 128 | bytes 1024 | tf_op jit(solution)/shard_map/psum | solution.py:77
  790.9 1.7 scatter_custom_fusion.2
  792.6 33.6 %all-gather.24.cloned.1.call-done = f32[4096,128]{1,0:T(8,128)} async-done(((f32[256,128]{1,0:T(8,128)}), f32[4096,128]{1,0:T(8,128)}) %all-gather.24.cloned.1.call-update) | async-done | bytes 2097168 | tf_op jit(solution)/shard_map/all_gather | solution.py:53
  826.2 6.3 fusion.49
  834.1 75.8 %all-gather.34.cloned.1.call-done = f32[96,24,128]{2,1,0:T(8,128)} async-done(((f32[6,24,128]{2,1,0:T(8,128)}), f32[96,24,128]{2,1,0:T(8,128)}) %all-gather.34.cloned.1.call-update) | async-done | bytes 1179664 | tf_op jit(solution)/shard_map/all_gather | solution.py:67
  911.4 78.5 %psum.61 = f32[128]{0:T(128)S(1)} all-reduce(f32[128]{0:T(128)S(1)} %get-tuple-element.13), channel_id=1, replica_groups=mesh['seg'=16,'sub'=16] {'seg','sub'}, use_global_device_ids=true, to_apply=%region_19.21 | all-reduce | flops 128 | bytes 1024 | tf_op jit(solution)/shard_map/psum | solution.py:93
  990.1 72.3 %psum.62 = f32[128]{0:T(128)S(1)} all-reduce(f32[128]{0:T(128)S(1)} %fusion.59), channel_id=1, replica_groups=mesh['seg'=16,'sub'=16] {'seg','sub'}, use_global_device_ids=true, to_apply=%region_21.23 | all-reduce | flops 128 | bytes 1024 | tf_op jit(solution)/shard_map/psum | solution.py:77
  1062.5 1.7 scatter_custom_fusion.3
  1064.2 33.6 %all-gather.26.cloned.1.call-done = f32[4096,128]{1,0:T(8,128)} async-done(((f32[256,128]{1,0:T(8,128)}), f32[4096,128]{1,0:T(8,128)}) %all-gather.26.cloned.1.call-update) | async-done | bytes 2097168 | tf_op jit(solution)/shard_map/all_gather | solution.py:53
  1097.8 6.3 fusion.52
  1105.6 75.8 %all-gather.36.cloned.1.call-done = f32[96,24,128]{2,1,0:T(8,128)} async-done(((f32[6,24,128]{2,1,0:T(8,128)}), f32[96,24,128]{2,1,0:T(8,128)}) %all-gather.36.cloned.1.call-update) | async-done | bytes 1179664 | tf_op jit(solution)/shard_map/all_gather | solution.py:67
  1183.0 78.3 %psum.63 = f32[128]{0:T(128)S(1)} all-reduce(f32[128]{0:T(128)S(1)} %multiply_reduce_fusion), channel_id=1, replica_groups=mesh['seg'=16,'sub'=16] {'seg','sub'}, use_global_device_ids=true, to_apply=%region_25.27 | all-reduce | flops 128 | bytes 1024 | tf_op jit(solution)/shard_map/psum | solution.py:93
  (80 shorter events, 17.1 us)
Async XLA Ops:
  7.2 39.7 %copy-start = (f32[128,256]{1,0:T(8,128)S(1)}, f32[128,256]{1,0:T(8,128)}, u32[]{:S(2)}) copy-start(f32[128,256]{1,0:T(8,128)} %param.14) | copy-start | bytes 393220
  7.2 110.9 %reduce-scatter.2.cloned.1.call-start = ((), (), s32[]{:S(2)}) async-start(), calls=%async_computation.1 | async-start | bytes 2228224 | tf_op jit(solution)/shard_map/reduce_scatter | solution.py:42
  46.8 71.3 %copy-start.1 = (s32[6,1,24]{2,1,0:T(1,128)S(1)}, s32[6,1,24]{2,1,0:T(1,128)}, u32[]{:S(2)}) copy-start(s32[6,1,24]{2,1,0:T(1,128)} %param.17) | copy-start | bytes 1732
  55.1 111.7 %copy-start.2 = (s32[6,16]{1,0:T(8,128)S(1)}, s32[6,16]{1,0:T(8,128)}, u32[]{:S(2)}) copy-start(s32[6,16]{1,0:T(8,128)} %param.16) | copy-start | bytes 1156
  55.1 103.8 %all-gather.18.cloned.1.call-start = ((), (), s32[]{:S(2)}) async-start(), calls=%async_computation.2 | async-start | bytes 2228224 | tf_op jit(solution)/shard_map/all_gather | solution.py:53
  118.1 124.4 %all-gather.28.cloned.1.call-start = ((), (), s32[]{:S(2)}) async-start(), calls=%async_computation.7 | async-start | bytes 1253376 | tf_op jit(solution)/shard_map/all_gather | solution.py:67
  166.7 116.6 %all-gather.20.cloned.1.call-start = ((), (), s32[]{:S(2)}) async-start(), calls=%async_computation.3 | async-start | bytes 2228224 | tf_op jit(solution)/shard_map/all_gather | solution.py:53
  245.8 121.2 %all-gather.30.cloned.1.call-start = ((), (), s32[]{:S(2)}) async-start(), calls=%async_computation.8 | async-start | bytes 1253376 | tf_op jit(solution)/shard_map/all_gather | solution.py:67
  291.1 263.7 %all-gather.22.cloned.1.call-start = ((), (), s32[]{:S(2)}) async-start(), calls=%async_computation.4 | async-start | bytes 2228224 | tf_op jit(solution)/shard_map/all_gather | solution.py:53
  521.2 117.2 %all-gather.32.cloned.1.call-start = ((), (), s32[]{:S(2)}) async-start(), calls=%async_computation.9 | async-start | bytes 1253376 | tf_op jit(solution)/shard_map/all_gather | solution.py:67
  562.6 263.6 %all-gather.24.cloned.1.call-start = ((), (), s32[]{:S(2)}) async-start(), calls=%async_computation.5 | async-start | bytes 2228224 | tf_op jit(solution)/shard_map/all_gather | solution.py:53
  792.6 117.2 %all-gather.34.cloned.1.call-start = ((), (), s32[]{:S(2)}) async-start(), calls=%async_computation.10 | async-start | bytes 1253376 | tf_op jit(solution)/shard_map/all_gather | solution.py:67
  834.0 263.8 %all-gather.26.cloned.1.call-start = ((), (), s32[]{:S(2)}) async-start(), calls=%async_computation.6 | async-start | bytes 2228224 | tf_op jit(solution)/shard_map/all_gather | solution.py:53
  1064.2 117.2 %all-gather.36.cloned.1.call-start = ((), (), s32[]{:S(2)}) async-start(), calls=%async_computation.11 | async-start | bytes 1253376 | tf_op jit(solution)/shard_map/all_gather | solution.py:67
Sparse Core Ops, SparseCore 0:
  55.2 62.8 reduce-scatter.1
  119.9 38.8 all-gather.17
  166.8 75.6 all-gather.27
  245.9 37.3 all-gather.19
  291.2 75.6 all-gather.29
  521.3 33.4 all-gather.21
  562.8 75.6 all-gather.31
  792.7 33.4 all-gather.23
  834.1 75.6 all-gather.33
  1064.3 33.4 all-gather.25
  1105.7 75.6 all-gather.35
where the time goes:
time: 1270 us
  waiting for transfers between devices  621 us (49%)
  blocking collectives  569 us (45%)
  matrix products  39.6 us (3%)
  other arithmetic  19.6 us (2%)
  between operations  14.1 us (1%)
    all_gather x5, waiting for transfers between devices, jump_of(): pieces = lax.all_gather(picked[None], 'sub', axis=0, tiled=True)  379 us
    psum x4, blocking collectives, squares(): return lax.psum(local_inner(residual, residual), ('seg', 'sub'))  295 us
    psum x3, blocking collectives, body(): curve = lax.psum(local_inner(direction, image_dual), ('seg', 'sub'))  235 us
    all_gather x5, waiting for transfers between devices, schur_apply(): lax.all_gather(trace_in, 'seg', axis=0, tiled=True)  179 us
    reduce_scatter x1, waiting for transfers between devices, body(): lax.psum_scatter(contract_segments(kernel_tile(all_mid, all_dir, seg_mid,...  62.9 us
    dot_general x5, matrix products, schur_apply(): jnp.dot(flex_rows, lax.all_gather(trace_in, 'seg', axis=0, tiled=True), p...  31.4 us
  transfers between devices with their start and end apart: 11, of which 11 were waited for; matrix products, arithmetic and copies ran while one was open for 0% of the time, Pallas kernels for 0%

commit v1 on v0

v1 whole, which is shorter than its diff:
```python
import jax
import jax.numpy as jnp
from jax import lax
from jax.experimental import pallas as pl
from jax.experimental.pallas import tpu as pltpu
from jax.sharding import PartitionSpec as P

ITERS = 4
ROUNDS = 6
SHARE = 24
PICKS = ROUNDS * SHARE
BAND = PICKS // 2
MSG = BAND + 8
ROWS = 256
LANES = 128
HALF = LANES // 2
CHIPS = 8
MAIN = CHIPS * LANES
DEPTH = CHIPS * PICKS
CORE2 = 0.05 * 0.05
f32 = jnp.float32
bf16 = jnp.bfloat16
MESH = pl.DeviceIdType.MESH

PLANE = ((0, 1), (1, 0), (-1, 0), (1, 1), (-1, 1), (2, 0), (2, 1))
NEAR = ((0, 1), (1, 0), (-1, 0), (1, 1), (-1, 1))
FAR = (3, -3)


def split2(value):
    high = value.astype(bf16)
    return high, (value - high.astype(f32)).astype(bf16)


def dot(a, b):
    return jnp.dot(a, b, preferred_element_type=f32)


def kernel(em, ed, sm, sv, cur, part, eb, flex,
           mult_out, trace_out,
           geo, cg, sg, xg, fg,
           wa0, wa1, wa2, wa3, wb0, wb1, wb2, wb3, fw, far_s, far_r, ffs, ffr,
           fv, fhi, flo, fsh, fsl, rem, kh, kl, cb, xb, pt, pk, ptb, pb, est, ebc,
           sgn, own, base, tr, ts, tp, car, vr, vs, vp, vx,
           fsem, gsend, grecv, dsend, drecv, ssend, srecv, nsend, nrecv, zsend, zrecv):
    seg = lax.axis_index("seg")
    sub = lax.axis_index("sub")
    x, ylo, c = seg // 4, (seg // 2) % 2, seg % 2
    z, yh = sub // 2, sub % 2
    q = seg // 2
    windows = ((wa0, wa1, wa2, wa3), (wb0, wb1, wb2, wb3))

    def plane_dev(dx, fy, fc):
        yy = 1 - ylo if fy else ylo
        cc = 1 - c if fc else c
        return (((x + dx + 4) % 4) * 4 + yy * 2 + cc, sub)

    def column_dev(dz, fy):
        yy = 1 - yh if fy else yh
        return (seg, ((z + dz + 8) % 8) * 2 + yy)

    def chip_from(dx, fy):
        yy = 1 - ylo if fy else ylo
        return ((x - dx + 4) % 4) * 2 + yy

    def remote(src, dst, ss, rs, dev):
        return pltpu.make_async_remote_copy(
            src_ref=src, dst_ref=dst, send_sem=ss, recv_sem=rs, device_id=dev, device_id_type=MESH)

    pending = []
    around = [(dx, fy, fc) for dx, fy in PLANE for fc in (0, 1)] + [(0, 0, 1)]

    def low_lanes(rows):
        return lax.broadcasted_iota(jnp.int32, (rows, LANES), 1) < HALF

    def swap(value):
        return pltpu.roll(value, HALF, 1)

    flex_copy = pltpu.make_async_copy(flex.at[0], fv, fsem)
    flex_copy.start()
    barrier = pltpu.get_barrier_semaphore()
    for dx, fy, fc in around:
        pl.semaphore_signal(barrier, inc=1, device_id=plane_dev(dx, fy, fc), device_id_type=MESH)
    for dz, fy in NEAR:
        pl.semaphore_signal(barrier, inc=1, device_id=column_dev(dz, fy), device_id_type=MESH)
    for dz in FAR:
        pl.semaphore_signal(barrier, inc=1, device_id=column_dev(dz, 0), device_id_type=MESH)
    geo[c, q, 0:3, :] = sm[...]
    geo[c, q, 3:6, :] = sv[...]
    geo[c, q, 6:8, :] = jnp.zeros((2, ROWS), f32)
    turned = cur[...].T
    left = low_lanes(LANES)
    cg[0, c, q] = jnp.where(left, turned[:LANES], swap(turned[LANES:]))
    cg[1, c, q] = jnp.where(left, swap(turned[:LANES]), turned[LANES:])
    pl.semaphore_wait(barrier, len(around) + len(NEAR) + len(FAR))

    geo_copies = []
    for k, (dx, fy, fc) in enumerate(around):
        copy = remote(geo.at[c, q], geo.at[c, q], gsend.at[k], grecv.at[k], plane_dev(dx, fy, fc))
        copy.start()
        geo_copies.append(copy)
    pending.extend(geo_copies)

    def gather_start(buf, g):
        mine = buf.at[c, q]
        for k, (dx, fy) in enumerate(PLANE):
            copy = remote(mine, mine, dsend.at[g, k], drecv.at[g, k], plane_dev(dx, fy, 0))
            copy.start()
            pending.append(copy)
        k = len(PLANE)
        copy = remote(mine, mine, ssend.at[g, k], srecv.at[g, k], plane_dev(0, 0, 1))
        copy.start()
        pending.append(copy)

    def gather_near(buf, g, each):
        each(c, q)
        for k, (dx, fy) in enumerate(PLANE):
            origin = chip_from(dx, fy)
            here = buf.at[c, origin]
            remote(here, here, dsend.at[g, k], drecv.at[g, k], plane_dev(0, 0, 1)).wait_recv()
            copy = remote(here, here, ssend.at[g, k], srecv.at[g, k], plane_dev(0, 0, 1))
            copy.start()
            pending.append(copy)
            each(c, origin)

    def gather_far(buf, g, each):
        for k, (dx, fy) in ((7, (0, 0)),) + tuple(enumerate(PLANE)):
            origin = chip_from(dx, fy)
            here = buf.at[1 - c, origin]
            remote(here, here, ssend.at[g, k], srecv.at[g, k], plane_dev(0, 0, 1)).wait_recv()
            each(1 - c, origin)

    gather_start(cg.at[0], 0)
    gather_start(cg.at[1], 1)

    lane_at = lax.broadcasted_iota(jnp.int32, (1, ROWS), 1)
    pt[...] = jnp.zeros((ROWS, ROWS), f32)
    pk[...] = jnp.zeros((ROWS, ROWS), f32)

    def hot_row(k, carry):
        row = jnp.where(lane_at == eb[k // SHARE, 0, k % SHARE], 1.0, 0.0).astype(f32)
        upper = k // BAND
        at = k - upper * BAND
        place = jnp.where(at < HALF, upper * HALF + at, LANES + upper * 8 + at - HALF)
        pt[pl.ds(k, 1), :] = row
        pk[pl.ds(place, 1), :] = row
        return carry
    lax.fori_loop(0, PICKS, hot_row, 0)
    ptb[...] = pt[0:PICKS, :].astype(bf16)
    pb[...] = pk[...].T

    est[...] = jnp.zeros((LANES, ROWS), f32)
    for comp in range(3):
        est[comp:comp + 1, :] = em[comp]
        est[3 + comp:4 + comp, :] = ed[comp]
    columns = est[...].T
    for comp in range(6):
        ebc[comp] = jnp.broadcast_to(columns[:, comp:comp + 1], (ROWS, LANES))

    left_band = low_lanes(SHARE)
    for b in range(3):
        band = slice(b * SHARE, (b + 1) * SHARE)
        first = jnp.where(part[b, sub] > sub, 1.0, 0.0).astype(f32)
        second = jnp.where(part[b + 3, sub] > sub, 1.0, 0.0).astype(f32)
        mark = jnp.where(left_band, first, second)
        own[band, :] = mark
        sgn[band, :] = mark * 2.0 - 1.0

    for k, (dx, fy, fc) in enumerate(around):
        geo_copies[k].wait_recv()

    def tile(step, carry):
        half, chip = step // CHIPS, step % CHIPS
        for h in range(2):
            row = [geo[half, chip, pl.ds(comp, 1), h * LANES:(h + 1) * LANES] for comp in range(6)]
            lanes = pl.ds(pl.multiple_of(chip * ROWS + h * LANES, LANES), LANES)
            for part_at in range(4):
                rows = slice(part_at * 64, part_at * 64 + 64)
                dist = jnp.full((64, LANES), CORE2, f32)
                along = jnp.zeros((64, LANES), f32)
                for comp in range(3):
                    gap = ebc[comp, rows, :] - row[comp]
                    dist = dist + gap * gap
                    along = along + ebc[3 + comp, rows, :] * row[3 + comp]
                high, low = split2(along * lax.rsqrt(dist))
                kh[half, rows, lanes] = high
                kl[half, rows, lanes] = low
        return carry
    lax.fori_loop(0, 2 * CHIPS, tile, 0)

    def unpack(value):
        high = value.astype(bf16).astype(f32)
        low = value - high
        side = low_lanes(value.shape[0])
        return jnp.where(side, high, swap(low)), jnp.where(side, swap(high), low)

    def dense_block(buf, h):
        def each(half, chip):
            one, two = unpack(buf[half, chip])
            cb[h, half, pl.ds(pl.multiple_of(chip * ROWS, LANES), LANES), :] = one.astype(bf16)
            cb[h, half, pl.ds(pl.multiple_of(chip * ROWS + LANES, LANES), LANES), :] = two.astype(bf16)
        return each

    def dense_dot(high, low, half, h):
        return dot(high[half], cb[h, half]) + dot(low[half], cb[h, half])

    def split_flex(step, carry):
        half, chip = step // CHIPS, step % CHIPS
        for h in range(2):
            src = pl.ds(pl.multiple_of((chip * 2 + half) * ROWS + h * LANES, LANES), LANES)
            dst = pl.ds(pl.multiple_of(chip * ROWS + h * LANES, LANES), LANES)
            high, low = split2(fv[:, src])
            fhi[half, :, dst] = high
            flo[half, :, dst] = low
        return carry

    def pick_columns(half):
        rem[...] = jnp.zeros((2, ROWS, LANES), f32)

        def one(chip, carry):
            tail = pltpu.roll(pb[:, LANES:], chip * (PICKS - LANES), 1)
            choose = jnp.concatenate([pb[:, :LANES], tail], axis=1).astype(bf16)
            src = pl.ds(pl.multiple_of(chip * ROWS, ROWS), ROWS)
            dst = pl.ds(pl.multiple_of(chip * LANES, LANES), LANES)
            for at, (whole, out) in enumerate(((fhi, fsh), (flo, fsl))):
                got = dot(whole[half, :, src], choose)
                out[half, :, dst] = got[:, :LANES].astype(bf16)
                rem[at] += got[:, LANES:]
            return carry
        lax.fori_loop(0, CHIPS, one, 0)
        fsh[half, :, MAIN:] = rem[0].astype(bf16)
        fsl[half, :, MAIN:] = rem[1].astype(bf16)

    def pick_rows(full):
        high = full.astype(bf16)
        rest = full - high.astype(f32)
        mid = rest.astype(bf16)
        low = (rest - mid.astype(f32)).astype(bf16)
        both = dot(ptb[...], jnp.where(low_lanes(ROWS), high.astype(f32), mid.astype(f32)).astype(bf16))
        picked = (both + swap(both)) + dot(ptb[...], low)
        return jnp.where(low_lanes(BAND), picked[:BAND], picked[BAND:])

    def near_slot(dz, fy):
        return (dz + 1) * 2 + fy

    def near_start(buf, e):
        mine = buf.at[near_slot(0, 0)]
        for k, (dz, fy) in enumerate(NEAR):
            copy = remote(mine, buf.at[near_slot(-dz, fy)], nsend.at[e, k], nrecv.at[e, k], column_dev(dz, fy))
            copy.start()
            pending.append(copy)

    def near_wait(buf, e):
        for k, (dz, fy) in enumerate(NEAR):
            here = buf.at[near_slot(-dz, fy)]
            remote(here, here, nsend.at[e, k], nrecv.at[e, k], column_dev(dz, fy)).wait_recv()

    def far_start(src, dst, e):
        for t, dz in enumerate(FAR):
            copy = remote(src.at[t], dst.at[t], zsend.at[e, t], zrecv.at[e, t], column_dev(dz, 0))
            copy.start()
            pending.append(copy)

    def far_wait(dst, e):
        for t, dz in enumerate(FAR):
            here = dst.at[t]
            remote(here, here, zsend.at[e, t], zrecv.at[e, t], column_dev(dz, 0)).wait_recv()

    def place_of(r, at):
        p = part[r, at]
        rel = (p // 2 - z + 8) % 8
        shifted = (rel + 1) % 8
        slot = shifted * 2 + jnp.where(p % 2 == yh, 0, 1)
        inside = shifted < 3
        return rel, inside, jnp.where(inside, slot, 0)

    far_places = [[place_of(r, ((z + dz + 8) % 8) * 2 + yh)[2] for r in range(ROUNDS)] for dz in FAR]
    my_places = [place_of(r, sub) for r in range(ROUNDS)]

    def sums_far(buf, dst, at):
        keep = [buf[s, at:at + 8, :] for s in range(6)]
        upper = (keep[2] + keep[3]) + (keep[4] + keep[5])
        whole = upper + (keep[0] + keep[1])
        dst[0, at:at + 8, :] = upper
        dst[1, at:at + 8, :] = whole
        return whole

    def sparse_block(buf, h):
        def each(half, chip):
            one, two = unpack(buf[half, chip, 0:BAND, :])
            for at, value in ((0, one), (HALF, two)):
                rows = pl.ds(pl.multiple_of(chip * LANES + at, HALF), HALF)
                xb[h, half, rows, :] = value[:HALF].astype(bf16)
            tail = pl.ds(pl.multiple_of(MAIN + chip * 16, 16), 16)
            xb[h, half, tail, :] = jnp.concatenate([one[HALF:], two[HALF:]], axis=0).astype(bf16)
        return each

    def sparse_dot(half, h):
        return dot(fsh[half], xb[h, half]) + dot(fsl[half], xb[h, half])

    zeros8 = jnp.zeros((8, LANES), f32)

    def inner_rows(residual, image):
        gamma = jnp.sum(own[...] * residual * residual, axis=0, keepdims=True)
        delta = jnp.sum(residual * image, axis=0, keepdims=True)
        return jnp.concatenate([gamma, delta, jnp.zeros((6, LANES), f32)], axis=0)

    def chain(h):
        cur_block, src_block = dense_block(cg.at[h], h), dense_block(sg.at[h], h)
        gather_near(cg.at[h], h, cur_block)
        yield
        total = dense_dot(kh, kl, c, h)
        gather_far(cg.at[h], h, cur_block)
        total = total + dense_dot(kh, kl, 1 - c, h)
        total = total + swap(total)
        sg[h, c, q] = jnp.where(left, total[:LANES], total[LANES:])
        gather_start(sg.at[h], 2 + h)
        yield
        gather_near(sg.at[h], 2 + h, src_block)
        yield
        total = dense_dot(fhi, flo, c, h)
        gather_far(sg.at[h], 2 + h, src_block)
        total = total + dense_dot(fhi, flo, 1 - c, h)
        total = total + swap(total)
        base[h] = total
        mine = pick_rows(total)
        scalars = zeros8
        gamma_was = alpha_was = None
        for g in range(ITERS + 1):
            e = g * 2 + h
            buf = windows[h][g] if g < ITERS else fw.at[h]
            if g == ITERS:
                buf[near_slot(0, 0)] = scalars
                near_start(buf, e)
                yield
                near_wait(buf, e)
                whole = sums_far(buf, ffs.at[h], 0)
                far_start(ffs.at[h], ffr.at[h], e)
                yield
                far_wait(ffr.at[h], e)
                fg[h, c, q] = whole + ffr[h, 0] + ffr[h, 1]
                gather_start(fg.at[h], 12 + h)
                yield
                gather_near(fg.at[h], 12 + h, lambda half, chip: None)
                yield
                gather_far(fg.at[h], 12 + h, lambda half, chip: None)
                sums = zeros8
                for half in range(2):
                    for chip in range(CHIPS):
                        sums = sums + fg[h, half, chip]
            else:
                buf[near_slot(0, 0), 0:BAND, :] = mine
                buf[near_slot(0, 0), BAND:MSG, :] = scalars
                near_start(buf, e)
                yield
                near_wait(buf, e)
                for t in range(2):
                    for b in range(3):
                        band = slice(b * SHARE, (b + 1) * SHARE)
                        far_s[e, t, band, :] = jnp.where(
                            left_band, buf[far_places[t][b], band, :], buf[far_places[t][b + 3], band, :])
                whole = sums_far(buf, far_s.at[e], BAND)
                far_start(far_s.at[e], far_r.at[e], e)
                yield
                far_wait(far_r.at[e], e)
                pieces = []
                for b in range(3):
                    band = slice(b * SHARE, (b + 1) * SHARE)
                    sides = []
                    for r in (b, b + 3):
                        rel, inside, slot = my_places[r]
                        away = jnp.where(rel < 5, far_r[e, 1, band, :], far_r[e, 0, band, :])
                        sides.append(jnp.where(inside, buf[slot, band, :], away))
                    pieces.append(mine[band, :] - jnp.where(left_band, sides[0], sides[1]))
                vector = jnp.concatenate(pieces, axis=0)
                xg[e, c, q, 0:BAND, :] = vector
                xg[e, c, q, BAND:MSG, :] = whole + far_r[e, 0, BAND:MSG, :] + far_r[e, 1, BAND:MSG, :]
                gather_start(xg.at[e], 4 + e)
                yield
                block = sparse_block(xg.at[e], h)
                gather_near(xg.at[e], 4 + e, block)
                yield
                total = sparse_dot(c, h)
                gather_far(xg.at[e], 4 + e, block)
                total = total + sparse_dot(1 - c, h)
                applied = total + swap(total)
                sums = zeros8
                for half in range(2):
                    for chip in range(CHIPS):
                        sums = sums + xg[e, half, chip, BAND:MSG, :]
            if g == 0:
                vr[h] = vector
                tr[h] = applied
                mine = pick_rows(applied)
                scalars = inner_rows(vector, mine)
                continue
            sums = sums + swap(sums)
            gamma, delta = sums[0:1], sums[1:2]
            residual = vr[h]
            if g == 1:
                alpha = gamma / delta
                step, direction = vector, residual
                step_image = applied
            else:
                beta = gamma / gamma_was
                alpha = gamma / (delta - beta * gamma / alpha_was)
                direction = residual + beta * vp[h]
                if g < ITERS:
                    step = vector + beta * vs[h]
                    step_image = applied + beta * ts[h]
            if g < ITERS:
                image = tr[h]
                fresh = image - alpha * step_image
                mine = pick_rows(fresh)
                residual = residual - alpha * step
                scalars = inner_rows(residual, mine)
                direction_image = image if g == 1 else image + beta * tp[h]
                vr[h] = residual
                vs[h] = step
                ts[h] = step_image
                tr[h] = fresh
                vp[h] = direction
                tp[h] = direction_image
                if g == 1:
                    vx[h] = alpha * direction
                    car[h] = alpha * direction_image
                else:
                    vx[h] += alpha * direction
                    car[h] += alpha * direction_image
            else:
                vx[h] += alpha * direction
                car[h] += alpha * (tr[h] + beta * tp[h])
            gamma_was, alpha_was = gamma, alpha

    chains = (chain(0), chain(1))

    def go(which):
        next(chains[which], None)

    go(0)
    go(0)
    go(1)
    go(1)
    flex_copy.wait()
    lax.fori_loop(0, 2 * CHIPS, split_flex, 0)
    go(0)
    go(0)
    go(1)
    go(1)
    go(0)
    pick_columns(0)
    go(1)
    pick_columns(1)
    go(0)
    go(1)
    go(0)
    go(0)
    go(1)
    go(1)
    for _ in range(ITERS):
        for which in (0, 1, 0, 1, 0, 0, 1, 1):
            go(which)

    side = low_lanes(ROWS)
    trace_out[0] = jnp.where(side, base[0] - car[0], base[1] - car[1])
    for b in range(3):
        band = slice(b * SHARE, (b + 1) * SHARE)
        lower, upper = vx[0, band, :], vx[1, band, :]
        sign = sgn[band, :]
        lower, upper = sign * lower, sign * upper
        mult_out[0, b] = jnp.where(left_band, lower, swap(upper))
        mult_out[0, b + 3] = jnp.where(left_band, swap(lower), upper)

    for copy in pending:
        copy.wait_send()


def body(edge_mid, edge_dir, seg_mid, seg_vec, currents, flexibility, partner, edge_block):
    vmem = pl.BlockSpec(memory_space=pltpu.VMEM)
    smem = pl.BlockSpec(memory_space=pltpu.SMEM)
    dma = pltpu.SemaphoreType.DMA
    half = CHIPS * ROWS

    def room(*shape):
        return pltpu.VMEM(shape, f32)

    def short(*shape):
        return pltpu.VMEM(shape, bf16)
    both = 2 * ITERS
    scratch = [
        room(2, CHIPS, 8, ROWS),
        room(2, 2, CHIPS, LANES, LANES),
        room(2, 2, CHIPS, LANES, LANES),
        room(both, 2, CHIPS, MSG, LANES),
        room(2, 2, CHIPS, 8, LANES),
    ]
    scratch += [room(6, MSG, LANES)] * both
    scratch += [room(2, 6, 8, LANES), room(both, 2, MSG, LANES), room(both, 2, MSG, LANES)]
    scratch += [room(2, 2, 8, LANES), room(2, 2, 8, LANES)]
    scratch += [
        room(ROWS, 2 * half), short(2, ROWS, half), short(2, ROWS, half),
        short(2, ROWS, DEPTH), short(2, ROWS, DEPTH), room(2, ROWS, LANES),
        short(2, ROWS, half), short(2, ROWS, half),
        short(2, 2, half, LANES), short(2, 2, DEPTH, LANES),
        room(ROWS, ROWS), room(ROWS, ROWS), short(PICKS, ROWS), room(ROWS, ROWS),
        room(LANES, ROWS), room(6, ROWS, LANES),
        room(BAND, LANES), room(BAND, LANES),
    ]
    scratch += [room(2, ROWS, LANES)] * 5
    scratch += [room(2, BAND, LANES)] * 4
    scratch += [
        dma, dma((15,)), dma((15,)),
        dma((14, 7)), dma((14, 7)), dma((14, 8)), dma((14, 8)),
        dma((10, 5)), dma((10, 5)), dma((10, 2)), dma((10, 2)),
    ]
    return pl.pallas_call(
        kernel,
        out_shape=(
            jax.ShapeDtypeStruct((1, ROUNDS, SHARE, LANES), f32),
            jax.ShapeDtypeStruct((1, ROWS, LANES), f32),
        ),
        in_specs=[vmem] * 5 + [smem] * 2 + [pl.BlockSpec(memory_space=pl.ANY)],
        out_specs=(vmem, vmem),
        scratch_shapes=scratch,
        compiler_params=pltpu.CompilerParams(
            collective_id=0, has_side_effects=True, vmem_limit_bytes=56 * 1024 * 1024),
        name="interface_cg",
    )(jnp.transpose(edge_mid, (1, 0, 2)), jnp.transpose(edge_dir, (1, 0, 2)),
      seg_mid, seg_vec, currents, partner, edge_block, flexibility)


def solution(mesh):
    in_specs = (
        P("sub", None, "seg"),
        P("sub", None, "seg"),
        P(None, "seg"),
        P(None, "seg"),
        P(None, "seg"),
        P("sub", "seg", None),
        P(),
        P(None, "sub", None),
    )
    out_specs = (P("sub", None, "seg", None), P("sub", "seg", None))
    return jax.shard_map(body, mesh=mesh, in_specs=in_specs, out_specs=out_specs, check_vma=False)
```

time: 1270 us -> 152 us (0.12)
  waiting for transfers between devices: 621 us -> 0 us
  blocking collectives: 569 us -> 0 us
  Pallas kernels: 0 us -> 148 us
  matrix products: 39.6 us -> 0 us
  other arithmetic: 19.6 us -> 0 us
  between operations: 14.1 us -> 0.64 us
    all_gather x10 -> x0, waiting for transfers between devices: 557 us -> none  [the longest x5 379 us: jump_of(): pieces = lax.all_gather(picked[None], 'sub', axis=0, tiled=True)]
    psum x7 -> x0, blocking collectives: 531 us -> none  [the longest x4 295 us: squares(): return lax.psum(local_inner(residual, residual), ('seg', 'sub'))]
    pallas_call x0 -> x1, Pallas kernels: none -> 148 us  [body(): pl.pallas_call(kernel, out_shape=(jax.ShapeDtypeStruct((1, ROUNDS, SHARE,...]
    reduce_scatter x1 -> x0, waiting for transfers between devices: 62.9 us -> none  [body(): lax.psum_scatter(contract_segments(kernel_tile(all_mid, all_dir, seg_mid,...]
    dot_general x6 -> x0, matrix products: 39.6 us -> none  [the longest x5 31.4 us: schur_apply(): jnp.dot(flex_rows, lax.all_gather(trace_in, 'seg', axis=0, tiled=True), p...]
    all_gather x2 -> x0, blocking collectives: 38 us -> none  [the longest x1 21.4 us: body(): lax.all_gather(my_mid, 'seg', axis=1, tiled=True)]
  transfers between devices with their start and end apart: 11 -> 0, of which waited for: 11 -> 0; matrix products, arithmetic and copies ran while one was open for 0% -> 0% of each run, Pallas kernels for 0% -> 0%
where the time goes in v1:
time: 152 us; the launch traced here: 151 us
  Pallas kernels  148 us (97%)
  local copies, waits for them, and re-layouts  3.09 us (2%)
    pallas_call x1, Pallas kernels, body(): pl.pallas_call(kernel, out_shape=(jax.ShapeDtypeStruct((1, ROUNDS, SHARE,...  148 us
    unnamed x2, local copies, waits for them, and re-layouts  3.09 us

profile of v1, /device:TPU:1, one launch (start us, length us, event | category | flops | bytes accessed | tf_op | source)
XLA Modules:
  0.0 151.4 jit_solution(10158920664485752856)
XLA Ops:
  0.6 147.7 %interface_cg.1 = (f32[1,6,24,128]{3,2,1,0:T(8,128)}, f32[1,256,128]{2,1,0:T(8,128)}) custom-call(f32[3,1,256]{2,1,0:T(1,128)} %bitcast.2, f32[3,1,256]{2,1,0:T(1,128)} %bitcast.3, f32[3,256]{1,0:T(4,128)} %sm.1, f32[3,256]{1,0:T(4,128)} %sv.1, f32[128,256]{1,0:T(8,128)} %cur.1, s32[6,16]{1,0:T(8,128)} %part.1, s32[6,1,24]{2,1,0:T(1,128)} %eb.1, ...), custom_call_target="tpu_custom_call" | custom-call | tf_op jit(solution)/shard_map/interface_cg/pallas_call | solution.py:516
  148.3 1.5 %copy.12 = f32[1,6,24,128]{3,2,1,0:T(8,128)} copy(f32[1,6,24,128]{3,2,1,0:T(8,128)} %get-tuple-element.4) | data formatting | bytes 147456
  149.8 1.6 %copy.13 = f32[1,256,128]{2,1,0:T(8,128)} copy(f32[1,256,128]{2,1,0:T(8,128)} %get-tuple-element.5) | data formatting | bytes 262144

commit v2 on v1

v2 whole, which is shorter than its diff:
```python
import jax
import jax.numpy as jnp
from jax import lax
from jax.experimental import pallas as pl
from jax.experimental.pallas import tpu as pltpu
from jax.sharding import PartitionSpec as P

ITERS = 4
ROUNDS = 6
SHARE = 24
PICKS = ROUNDS * SHARE
BAND = PICKS // 2
MSG = BAND + 8
ROWS = 256
LANES = 128
HALF = LANES // 2
CHIPS = 8
MAIN = CHIPS * LANES
DEPTH = CHIPS * PICKS
CORE2 = 0.05 * 0.05
f32 = jnp.float32
bf16 = jnp.bfloat16
MESH = pl.DeviceIdType.MESH

PLANE = ((0, 1), (1, 0), (-1, 0), (1, 1), (-1, 1), (2, 0), (2, 1))
NEAR = ((0, 1), (1, 0), (-1, 0), (1, 1), (-1, 1))
FAR = (3, -3)
COLUMN = tuple((dz, fy) for dz in (4, -3, 3, -2, 2, -1, 1, 0) for fy in (1, 0) if dz or fy)


def split2(value):
    high = value.astype(bf16)
    return high, (value - high.astype(f32)).astype(bf16)


def dot(a, b):
    return jnp.dot(a, b, preferred_element_type=f32)


def kernel(em, ed, sm, sv, cur, part, eb, flex,
           mult_out, trace_out,
           geo, ge, cg, sg, xg, fg, ps, pr, pps, ppr, fps, fpr,
           wa0, wa1, wa2, wa3, wb0, wb1, wb2, wb3, fw, far_s, far_r,
           fv, fhi, flo, fsh, fsl, fssh, fssl, rem, kh, kl, cb, xb, pt, pk, ptb, pb, est, ebc,
           sgn, own, base, tx, tr, tp, trp, tsp, vr, vs, vp, vx,
           fsem, fsend, frecv, esend, erecv, gsend, grecv, dsend, drecv, psend, precv,
           nsend, nrecv, zsend, zrecv, asend, arecv):
    seg = lax.axis_index("seg")
    sub = lax.axis_index("sub")
    x, ylo, c = seg // 4, (seg // 2) % 2, seg % 2
    z, yh = sub // 2, sub % 2
    q = seg // 2
    windows = ((wa0, wa1, wa2, wa3), (wb0, wb1, wb2, wb3))

    def plane_dev(dx, fy, fc):
        yy = 1 - ylo if fy else ylo
        cc = 1 - c if fc else c
        return (((x + dx + 4) % 4) * 4 + yy * 2 + cc, sub)

    def column_dev(dz, fy):
        yy = 1 - yh if fy else yh
        return (seg, ((z + dz + 8) % 8) * 2 + yy)

    def chip_from(dx, fy):
        yy = 1 - ylo if fy else ylo
        return ((x - dx + 4) % 4) * 2 + yy

    def remote(src, dst, ss, rs, dev):
        return pltpu.make_async_remote_copy(
            src_ref=src, dst_ref=dst, send_sem=ss, recv_sem=rs, device_id=dev, device_id_type=MESH)

    pending = []
    sibling = plane_dev(0, 0, 1)

    def low_lanes(rows):
        return lax.broadcasted_iota(jnp.int32, (rows, LANES), 1) < HALF

    def swap(value):
        return pltpu.roll(value, HALF, 1)

    flex_copies = []
    for chip in range(CHIPS):
        src = flex.at[0, :, pl.ds(pl.multiple_of((chip * 2 + c) * ROWS, ROWS), ROWS)]
        copy = pltpu.make_async_copy(src, fv.at[c, :, chip * ROWS:(chip + 1) * ROWS], fsem.at[chip])
        copy.start()
        flex_copies.append(copy)
    barrier = pltpu.get_barrier_semaphore()
    peers = [plane_dev(dx, fy, 0) for dx, fy in PLANE] + [sibling]
    peers += [column_dev(dz, fy) for dz, fy in COLUMN]
    for peer in peers:
        pl.semaphore_signal(barrier, inc=1, device_id=peer, device_id_type=MESH)
    geo[q, 0:3, :] = sm[...]
    geo[q, 3:6, :] = sv[...]
    geo[q, 6:8, :] = jnp.zeros((2, ROWS), f32)
    for comp in range(3):
        ge[c, comp:comp + 1, :] = em[comp]
        ge[c, 3 + comp:4 + comp, :] = ed[comp]
    ge[c, 6:8, :] = jnp.zeros((2, ROWS), f32)
    turned = cur[...].T
    left = low_lanes(LANES)
    cg[0, q] = jnp.where(left, turned[:LANES], swap(turned[LANES:]))
    cg[1, q] = jnp.where(left, swap(turned[:LANES]), turned[LANES:])
    pl.semaphore_wait(barrier, len(peers))

    edge_copy = remote(ge.at[c], ge.at[c], esend, erecv, sibling)
    edge_copy.start()
    pending.append(edge_copy)
    geo_copies = []
    for k, (dx, fy) in enumerate(PLANE):
        copy = remote(geo.at[q], geo.at[q], gsend.at[k], grecv.at[k], plane_dev(dx, fy, 0))
        copy.start()
        geo_copies.append(copy)
    pending.extend(geo_copies)

    def gather_start(buf, g):
        mine = buf.at[q]
        for k, (dx, fy) in enumerate(PLANE):
            copy = remote(mine, mine, dsend.at[g, k], drecv.at[g, k], plane_dev(dx, fy, 0))
            copy.start()
            pending.append(copy)

    def gather_wait(buf, g, each):
        each(q)
        for k, (dx, fy) in enumerate(PLANE):
            origin = chip_from(dx, fy)
            here = buf.at[origin]
            remote(here, here, dsend.at[g, k], drecv.at[g, k], sibling).wait_recv()
            each(origin)

    gather_start(cg.at[0], 0)
    gather_start(cg.at[1], 1)
    shared_copies = []
    for chip in range(CHIPS):
        src = flex.at[0, :, pl.ds(pl.multiple_of((chip * 2 + 1 - c) * ROWS, ROWS), ROWS)]
        dst = fv.at[c, :, chip * ROWS:(chip + 1) * ROWS]
        copy = remote(src, dst, fsend.at[chip], frecv.at[chip], sibling)
        copy.start()
        shared_copies.append(copy)
    pending.extend(shared_copies)

    lane_at = lax.broadcasted_iota(jnp.int32, (1, ROWS), 1)
    pt[...] = jnp.zeros((ROWS, ROWS), f32)
    pk[...] = jnp.zeros((ROWS, ROWS), f32)

    def hot_row(k, carry):
        row = jnp.where(lane_at == eb[k // SHARE, 0, k % SHARE], 1.0, 0.0).astype(f32)
        upper = k // BAND
        at = k - upper * BAND
        place = jnp.where(at < HALF, upper * HALF + at, LANES + upper * 8 + at - HALF)
        pt[pl.ds(k, 1), :] = row
        pk[pl.ds(place, 1), :] = row
        return carry
    lax.fori_loop(0, PICKS, hot_row, 0)
    ptb[...] = pt[0:PICKS, :].astype(bf16)
    pb[...] = pk[...].T

    edge_copy.wait_recv()
    for side in range(2):
        est[...] = jnp.zeros((LANES, ROWS), f32)
        est[0:8, :] = ge[side]
        columns = est[...].T
        for comp in range(6):
            ebc[side, comp] = jnp.broadcast_to(columns[:, comp:comp + 1], (ROWS, LANES))

    left_band = low_lanes(SHARE)
    for b in range(3):
        band = slice(b * SHARE, (b + 1) * SHARE)
        first = jnp.where(part[b, sub] > sub, 1.0, 0.0).astype(f32)
        second = jnp.where(part[b + 3, sub] > sub, 1.0, 0.0).astype(f32)
        mark = jnp.where(left_band, first, second)
        own[band, :] = mark
        sgn[band, :] = mark * 2.0 - 1.0

    for copy in geo_copies:
        copy.wait_recv()

    def tile(step, carry):
        side, chip = step // CHIPS, step % CHIPS
        for h in range(2):
            row = [geo[chip, pl.ds(comp, 1), h * LANES:(h + 1) * LANES] for comp in range(6)]
            lanes = pl.ds(pl.multiple_of(chip * ROWS + h * LANES, LANES), LANES)
            for part_at in range(4):
                rows = slice(part_at * 64, part_at * 64 + 64)
                dist = jnp.full((64, LANES), CORE2, f32)
                along = jnp.zeros((64, LANES), f32)
                for comp in range(3):
                    gap = ebc[side, comp, rows, :] - row[comp]
                    dist = dist + gap * gap
                    along = along + ebc[side, 3 + comp, rows, :] * row[3 + comp]
                high, low = split2(along * lax.rsqrt(dist))
                kh[side, rows, lanes] = high
                kl[side, rows, lanes] = low
        return carry
    lax.fori_loop(0, 2 * CHIPS, tile, 0)

    def unpack(value):
        high = value.astype(bf16).astype(f32)
        low = value - high
        side = low_lanes(value.shape[0])
        return jnp.where(side, high, swap(low)), jnp.where(side, swap(high), low)

    def dense_block(buf, h):
        def each(chip):
            one, two = unpack(buf[chip])
            cb[h, pl.ds(pl.multiple_of(chip * ROWS, LANES), LANES), :] = one.astype(bf16)
            cb[h, pl.ds(pl.multiple_of(chip * ROWS + LANES, LANES), LANES), :] = two.astype(bf16)
        return each

    def dense_dot(high, low, h):
        def rows_of(side):
            return dot(high[side], cb[h]) + dot(low[side], cb[h])
        return rows_of

    def combine(inst, rows_of, scalars):
        other = rows_of(1 - c)
        other = other + swap(other)
        ps[inst, 0:LANES, :] = jnp.where(left, other[:LANES], other[LANES:])
        ps[inst, LANES:LANES + 8, :] = scalars
        copy = remote(ps.at[inst], pr.at[inst], psend.at[inst], precv.at[inst], sibling)
        copy.start()
        pending.append(copy)
        mine = rows_of(c)
        mine = mine + swap(mine)
        copy.wait_recv()
        got = pr[inst, 0:LANES, :]
        back = swap(got)
        top = mine[:LANES] + jnp.where(left, got, back)
        bottom = mine[LANES:] + jnp.where(left, back, got)
        return jnp.concatenate([top, bottom], axis=0), scalars + pr[inst, LANES:LANES + 8, :]

    def split_flex(step, carry):
        side, chip = step // CHIPS, step % CHIPS
        for h in range(2):
            lanes = pl.ds(pl.multiple_of(chip * ROWS + h * LANES, LANES), LANES)
            high, low = split2(fv[side, :, lanes])
            fhi[side, :, lanes] = high
            flo[side, :, lanes] = low
        return carry

    def pick_columns(half):
        rem[...] = jnp.zeros((2, ROWS, LANES), f32)

        def one(chip, carry):
            tail = pltpu.roll(pb[:, LANES:], chip * (PICKS - LANES), 1)
            choose = jnp.concatenate([pb[:, :LANES], tail], axis=1).astype(bf16)
            src = pl.ds(pl.multiple_of(chip * ROWS, ROWS), ROWS)
            dst = pl.ds(pl.multiple_of(chip * LANES, LANES), LANES)
            for at, (whole, out) in enumerate(((fhi, fsh), (flo, fsl))):
                got = dot(whole[half, :, src], choose)
                out[half, :, dst] = got[:, :LANES].astype(bf16)
                rem[at] += got[:, LANES:]
            return carry
        lax.fori_loop(0, CHIPS, one, 0)
        fsh[half, :, MAIN:] = rem[0].astype(bf16)
        fsl[half, :, MAIN:] = rem[1].astype(bf16)
        fssh[half] = dot(ptb[...], fsh[half]).astype(bf16)
        fssl[half] = dot(ptb[...], fsl[half]).astype(bf16)

    def pick_rows(full):
        high = full.astype(bf16)
        rest = full - high.astype(f32)
        mid = rest.astype(bf16)
        low = (rest - mid.astype(f32)).astype(bf16)
        both = dot(ptb[...], jnp.where(low_lanes(ROWS), high.astype(f32), mid.astype(f32)).astype(bf16))
        picked = (both + swap(both)) + dot(ptb[...], low)
        return jnp.where(low_lanes(BAND), picked[:BAND], picked[BAND:])

    def near_slot(dz, fy):
        return (dz + 1) * 2 + fy

    def near_start(buf, e):
        mine = buf.at[near_slot(0, 0)]
        for k, (dz, fy) in enumerate(NEAR):
            copy = remote(mine, buf.at[near_slot(-dz, fy)], nsend.at[e, k], nrecv.at[e, k], column_dev(dz, fy))
            copy.start()
            pending.append(copy)

    def near_wait(buf, e):
        for k, (dz, fy) in enumerate(NEAR):
            here = buf.at[near_slot(-dz, fy)]
            remote(here, here, nsend.at[e, k], nrecv.at[e, k], column_dev(dz, fy)).wait_recv()

    def far_start(src, dst, e):
        for t, dz in enumerate(FAR):
            copy = remote(src.at[t], dst.at[t], zsend.at[e, t], zrecv.at[e, t], column_dev(dz, 0))
            copy.start()
            pending.append(copy)

    def far_wait(dst, e):
        for t, dz in enumerate(FAR):
            here = dst.at[t]
            remote(here, here, zsend.at[e, t], zrecv.at[e, t], column_dev(dz, 0)).wait_recv()

    def place_of(r, at):
        p = part[r, at]
        rel = (p // 2 - z + 8) % 8
        shifted = (rel + 1) % 8
        slot = shifted * 2 + jnp.where(p % 2 == yh, 0, 1)
        inside = shifted < 3
        return rel, inside, jnp.where(inside, slot, 0)

    far_places = [[place_of(r, ((z + dz + 8) % 8) * 2 + yh)[2] for r in range(ROUNDS)] for dz in FAR]
    my_places = [place_of(r, sub) for r in range(ROUNDS)]

    def sums_far(buf, dst, at):
        keep = [buf[s, at:at + 8, :] for s in range(6)]
        upper = (keep[2] + keep[3]) + (keep[4] + keep[5])
        whole = upper + (keep[0] + keep[1])
        dst[0, at:at + 8, :] = upper
        dst[1, at:at + 8, :] = whole
        return whole

    def sparse_write(packed, chip, h):
        one, two = unpack(packed)
        for at, value in ((0, one), (HALF, two)):
            rows = pl.ds(pl.multiple_of(chip * LANES + at, HALF), HALF)
            xb[h, rows, :] = value[:HALF].astype(bf16)
        tail = pl.ds(pl.multiple_of(MAIN + chip * 16, 16), 16)
        xb[h, tail, :] = jnp.concatenate([one[HALF:], two[HALF:]], axis=0).astype(bf16)

    def sparse_block(buf, h):
        def each(chip):
            sparse_write(buf[chip, 0:BAND, :], chip, h)
        return each

    def sparse_dot(h):
        def rows_of(side):
            return dot(fsh[side], xb[h]) + dot(fsl[side], xb[h])
        return rows_of

    def combine_picks(inst, h, scalars):
        left_pack = low_lanes(BAND)

        def rows_of(side):
            got = dot(fssh[side], xb[h]) + dot(fssl[side], xb[h])
            got = got + swap(got)
            return jnp.where(left_pack, got[:BAND], got[BAND:])
        pps[inst, 0:BAND, :] = rows_of(1 - c)
        pps[inst, BAND:MSG, :] = scalars
        copy = remote(pps.at[inst], ppr.at[inst], psend.at[inst], precv.at[inst], sibling)
        copy.start()
        pending.append(copy)
        mine = rows_of(c)
        copy.wait_recv()
        return mine + ppr[inst, 0:BAND, :], scalars + ppr[inst, BAND:MSG, :]

    def add(first, second, scale):
        out = dict(first)
        for key, value in second.items():
            out[key] = out[key] + scale * value if key in out else scale * value
        return out

    def full_rows(inst, h, weights):
        for chip in range(CHIPS):
            value = None
            for g, weight in weights.items():
                term = weight * xg[g * 2 + h, chip, 0:BAND, :]
                value = term if value is None else value + term
            sparse_write(value, chip, h)
        return combine(inst, sparse_dot(h), zeros8)[0]

    zeros8 = jnp.zeros((8, LANES), f32)

    def inner_rows(residual, image):
        gamma = jnp.sum(own[...] * residual * residual, axis=0, keepdims=True)
        delta = jnp.sum(residual * image, axis=0, keepdims=True)
        return jnp.concatenate([gamma, delta, jnp.zeros((6, LANES), f32)], axis=0)

    def chain(h):
        gather_wait(cg.at[h], h, dense_block(cg.at[h], h))
        yield
        total, _ = combine(h, dense_dot(kh, kl, h), zeros8)
        sg[h, q] = jnp.where(left, total[:LANES], total[LANES:])
        gather_start(sg.at[h], 2 + h)
        yield
        gather_wait(sg.at[h], 2 + h, dense_block(sg.at[h], h))
        yield
        total, _ = combine(2 + h, dense_dot(fhi, flo, h), zeros8)
        base[h] = total
        mine = pick_rows(total)
        scalars = zeros8
        gamma_was = alpha_was = None
        for g in range(ITERS + 1):
            e = g * 2 + h
            if g == ITERS:
                fw[h, len(COLUMN)] = scalars
                for k, (dz, fy) in enumerate(COLUMN):
                    copy = remote(fw.at[h, len(COLUMN)], fw.at[h, k], asend.at[h, k], arecv.at[h, k], column_dev(dz, fy))
                    copy.start()
                    pending.append(copy)
                yield
                tx[h] = full_rows(12 + 3 * h, h, wx)
                tr[h] = full_rows(13 + 3 * h, h, wr)
                tp[h] = full_rows(14 + 3 * h, h, wp)
                yield
                sums = scalars
                for k, (dz, fy) in enumerate(COLUMN):
                    here = fw.at[h, k]
                    remote(here, here, asend.at[h, k], arecv.at[h, k], column_dev(dz, fy)).wait_recv()
                    sums = sums + fw[h, k]
                fg[h, q] = sums
                gather_start(fg.at[h], 12 + h)
                yield
                gather_wait(fg.at[h], 12 + h, lambda chip: None)
                sums = zeros8
                for chip in range(CHIPS):
                    sums = sums + fg[h, chip]
                fps[h] = sums
                copy = remote(fps.at[h], fpr.at[h], psend.at[18 + h], precv.at[18 + h], sibling)
                copy.start()
                pending.append(copy)
                yield
                copy.wait_recv()
                sums = sums + fpr[h]
            else:
                buf = windows[h][g]
                buf[near_slot(0, 0), 0:BAND, :] = mine
                buf[near_slot(0, 0), BAND:MSG, :] = scalars
                near_start(buf, e)
                yield
                near_wait(buf, e)
                for t in range(2):
                    for b in range(3):
                        band = slice(b * SHARE, (b + 1) * SHARE)
                        far_s[e, t, band, :] = jnp.where(
                            left_band, buf[far_places[t][b], band, :], buf[far_places[t][b + 3], band, :])
                whole = sums_far(buf, far_s.at[e], BAND)
                far_start(far_s.at[e], far_r.at[e], e)
                yield
                far_wait(far_r.at[e], e)
                pieces = []
                for b in range(3):
                    band = slice(b * SHARE, (b + 1) * SHARE)
                    sides = []
                    for r in (b, b + 3):
                        rel, inside, slot = my_places[r]
                        away = jnp.where(rel < 5, far_r[e, 1, band, :], far_r[e, 0, band, :])
                        sides.append(jnp.where(inside, buf[slot, band, :], away))
                    pieces.append(mine[band, :] - jnp.where(left_band, sides[0], sides[1]))
                vector = jnp.concatenate(pieces, axis=0)
                xg[e, q, 0:BAND, :] = vector
                xg[e, q, BAND:MSG, :] = whole + far_r[e, 0, BAND:MSG, :] + far_r[e, 1, BAND:MSG, :]
                gather_start(xg.at[e], 4 + e)
                yield
                gather_wait(xg.at[e], 4 + e, sparse_block(xg.at[e], h))
                yield
                sums = zeros8
                for chip in range(CHIPS):
                    sums = sums + xg[e, chip, BAND:MSG, :]
                applied, sums = combine_picks(4 + e, h, sums)
            if g == 0:
                vr[h] = vector
                trp[h] = applied
                mine = applied
                scalars = inner_rows(vector, mine)
                wr = {0: jnp.ones((1, LANES), f32)}
                continue
            sums = sums + swap(sums)
            gamma, delta = sums[0:1], sums[1:2]
            residual = vr[h]
            if g == 1:
                alpha = gamma / delta
                step, direction, step_image = vector, residual, applied
                wp, ws = wr, {}
            else:
                beta = gamma / gamma_was
                alpha = gamma / (delta - beta * gamma / alpha_was)
                direction = residual + beta * vp[h]
                if g < ITERS:
                    step = vector + beta * vs[h]
                    step_image = applied + beta * tsp[h]
                    wp = add(wr, wp, beta)
                    ws = add({}, ws, beta)
            if g < ITERS:
                mine = trp[h] - alpha * step_image
                residual = residual - alpha * step
                scalars = inner_rows(residual, mine)
                ws[g] = jnp.ones((1, LANES), f32)
                wx = add(wx if g > 1 else {}, wp, alpha)
                wr = add(wr, ws, -alpha)
                vr[h] = residual
                vs[h] = step
                vp[h] = direction
                trp[h] = mine
                tsp[h] = step_image
                vx[h] = alpha * direction if g == 1 else vx[h] + alpha * direction
            else:
                vx[h] += alpha * direction
                base[h] = base[h] - (tx[h] + alpha * (tr[h] + beta * tp[h]))
            gamma_was, alpha_was = gamma, alpha

    chains = (chain(0), chain(1))

    def go(which):
        next(chains[which], None)

    go(0)
    go(0)
    go(1)
    go(1)
    for copy in flex_copies:
        copy.wait()
    for copy in shared_copies:
        copy.wait_recv()
    lax.fori_loop(0, 2 * CHIPS, split_flex, 0)
    go(0)
    go(0)
    go(1)
    go(1)
    go(0)
    pick_columns(0)
    go(1)
    pick_columns(1)
    go(0)
    go(1)
    go(0)
    go(0)
    go(1)
    go(1)
    for _ in range(ITERS - 2):
        for which in (0, 1, 0, 1, 0, 0, 1, 1):
            go(which)
    for which in (0, 1, 0, 1, 0, 0, 0, 1, 1, 0, 1, 1, 0, 0, 1, 1):
        go(which)

    side = low_lanes(ROWS)
    trace_out[0] = jnp.where(side, base[0], base[1])
    for b in range(3):
        band = slice(b * SHARE, (b + 1) * SHARE)
        lower, upper = vx[0, band, :], vx[1, band, :]
        sign = sgn[band, :]
        lower, upper = sign * lower, sign * upper
        mult_out[0, b] = jnp.where(left_band, lower, swap(upper))
        mult_out[0, b + 3] = jnp.where(left_band, swap(lower), upper)

    for copy in pending:
        copy.wait_send()


def settle(mult, trace, mult_out, trace_out):
    mult_out[...] = mult[...]
    trace_out[...] = trace[...]


def body(edge_mid, edge_dir, seg_mid, seg_vec, currents, flexibility, partner, edge_block):
    vmem = pl.BlockSpec(memory_space=pltpu.VMEM)
    smem = pl.BlockSpec(memory_space=pltpu.SMEM)
    dma = pltpu.SemaphoreType.DMA
    half = CHIPS * ROWS

    def room(*shape):
        return pltpu.VMEM(shape, f32)

    def short(*shape):
        return pltpu.VMEM(shape, bf16)
    both = 2 * ITERS
    scratch = [
        room(CHIPS, 8, ROWS), room(2, 8, ROWS),
        room(2, CHIPS, LANES, LANES),
        room(2, CHIPS, LANES, LANES),
        room(both, CHIPS, MSG, LANES),
        room(2, CHIPS, 8, LANES),
        room(18, LANES + 8, LANES), room(18, LANES + 8, LANES),
        room(12, MSG, LANES), room(12, MSG, LANES), room(2, 8, LANES), room(2, 8, LANES),
    ]
    scratch += [room(6, MSG, LANES)] * both
    scratch += [room(2, 16, 8, LANES), room(both, 2, MSG, LANES), room(both, 2, MSG, LANES)]
    scratch += [
        room(2, ROWS, half), short(2, ROWS, half), short(2, ROWS, half),
        short(2, ROWS, DEPTH), short(2, ROWS, DEPTH),
        short(2, PICKS, DEPTH), short(2, PICKS, DEPTH), room(2, ROWS, LANES),
        short(2, ROWS, half), short(2, ROWS, half),
        short(2, half, LANES), short(2, DEPTH, LANES),
        room(ROWS, ROWS), room(ROWS, ROWS), short(PICKS, ROWS), room(ROWS, ROWS),
        room(LANES, ROWS), room(2, 6, ROWS, LANES),
        room(BAND, LANES), room(BAND, LANES),
    ]
    scratch += [room(2, ROWS, LANES)] * 4
    scratch += [room(2, BAND, LANES)] * 6
    scratch += [
        dma((8,)), dma((8,)), dma((8,)), dma, dma, dma((7,)), dma((7,)),
        dma((14, 7)), dma((14, 7)), dma((20,)), dma((20,)),
        dma((8, 5)), dma((8, 5)), dma((8, 2)), dma((8, 2)), dma((2, 15)), dma((2, 15)),
    ]
    outs = (
        jax.ShapeDtypeStruct((1, ROUNDS, SHARE, LANES), f32),
        jax.ShapeDtypeStruct((1, ROWS, LANES), f32),
    )
    solved = pl.pallas_call(
        kernel,
        out_shape=outs,
        in_specs=[vmem] * 5 + [smem] * 2 + [pl.BlockSpec(memory_space=pl.ANY)],
        out_specs=(vmem, vmem),
        scratch_shapes=scratch,
        compiler_params=pltpu.CompilerParams(
            collective_id=0, has_side_effects=True, vmem_limit_bytes=56 * 1024 * 1024),
        name="interface_cg",
    )(jnp.transpose(edge_mid, (1, 0, 2)), jnp.transpose(edge_dir, (1, 0, 2)),
      seg_mid, seg_vec, currents, partner, edge_block, flexibility)
    return pl.pallas_call(
        settle,
        out_shape=outs,
        in_specs=[vmem] * 2,
        out_specs=(vmem, vmem),
        name="settle",
    )(*solved)


def solution(mesh):
    in_specs = (
        P("sub", None, "seg"),
        P("sub", None, "seg"),
        P(None, "seg"),
        P(None, "seg"),
        P(None, "seg"),
        P("sub", "seg", None),
        P(),
        P(None, "sub", None),
    )
    out_specs = (P("sub", None, "seg", None), P("sub", "seg", None))
    return jax.shard_map(body, mesh=mesh, in_specs=in_specs, out_specs=out_specs, check_vma=False)
```

time: 152 us -> 152 us (level)
  local copies, waits for them, and re-layouts: 3.09 us -> 0 us
  Pallas kernels: 148 us -> 151 us
    pallas_call x1 -> x2, Pallas kernels: 148 us -> 151 us  [the longest x1 149 us: body(): pl.pallas_call(kernel, out_shape=outs, in_specs=[vmem] * 5 + [smem] * 2 +...]
    unnamed x2 -> x0, local copies, waits for them, and re-layouts: 3.09 us -> none
where the time goes in v2:
time: 152 us
  Pallas kernels  151 us (99%)
    pallas_call x1, Pallas kernels, body(): pl.pallas_call(kernel, out_shape=outs, in_specs=[vmem] * 5 + [smem] * 2 +...  149 us

profile of v2, /device:TPU:1, one launch (start us, length us, event | category | flops | bytes accessed | tf_op | source)
XLA Modules:
  0.0 151.6 jit_solution(14871868711454879686)
XLA Ops:
  0.6 149.3 %interface_cg.1 = (f32[1,6,24,128]{3,2,1,0:T(8,128)}, f32[1,256,128]{2,1,0:T(8,128)}) custom-call(f32[3,1,256]{2,1,0:T(1,128)} %bitcast.2, f32[3,1,256]{2,1,0:T(1,128)} %bitcast.3, f32[3,256]{1,0:T(4,128)} %sm.1, f32[3,256]{1,0:T(4,128)} %sv.1, f32[128,256]{1,0:T(8,128)} %cur.1, s32[6,16]{1,0:T(8,128)} %part.1, s32[6,1,24]{2,1,0:T(1,128)} %eb.1, ...), custom_call_target="tpu_custom_call" | custom-call | tf_op jit(solution)/shard_map/interface_cg/pallas_call | solution.py:589
  150.0 1.6 %settle.1 = (f32[1,6,24,128]{3,2,1,0:T(8,128)}, f32[1,256,128]{2,1,0:T(8,128)}) custom-call(f32[1,6,24,128]{3,2,1,0:T(8,128)} %get-tuple-element.4.mult, f32[1,256,128]{2,1,0:T(8,128)} %get-tuple-element.5.trace), custom_call_target="tpu_custom_call" | custom-call | tf_op jit(solution)/shard_map/settle/pallas_call | solution.py:600

commit v3 on v2

--- a/solution.py
+++ b/solution.py
@@ -494,10 +494,6 @@
     def go(which):
         next(chains[which], None)
 
-    go(0)
-    go(0)
-    go(1)
-    go(1)
     for copy in flex_copies:
         copy.wait()
     for copy in shared_copies:
@@ -505,18 +501,12 @@
     lax.fori_loop(0, 2 * CHIPS, split_flex, 0)
     go(0)
     go(0)
+    pick_columns(0)
     go(1)
     go(1)
-    go(0)
-    pick_columns(0)
-    go(1)
     pick_columns(1)
-    go(0)
-    go(1)
-    go(0)
-    go(0)
-    go(1)
-    go(1)
+    for which in (0, 0, 1, 1, 0, 1, 0, 1, 0, 0, 1, 1):
+        go(which)
     for _ in range(ITERS - 2):
         for which in (0, 1, 0, 1, 0, 0, 1, 1):
             go(which)

time: 152 us -> 151 us (level)
  no operation moved by 1% of the time
where the time goes in v3:
time: 151 us
  Pallas kernels  150 us (99%)
    pallas_call x1, Pallas kernels, body(): pl.pallas_call(kernel, out_shape=outs, in_specs=[vmem] * 5 + [smem] * 2 +...  149 us

profile of v3, /device:TPU:1, one launch (start us, length us, event | category | flops | bytes accessed | tf_op | source)
XLA Modules:
  0.0 151.0 jit_solution(14990012499799818572)
XLA Ops:
  0.6 148.7 %interface_cg.1 = (f32[1,6,24,128]{3,2,1,0:T(8,128)}, f32[1,256,128]{2,1,0:T(8,128)}) custom-call(f32[3,1,256]{2,1,0:T(1,128)} %bitcast.2, f32[3,1,256]{2,1,0:T(1,128)} %bitcast.3, f32[3,256]{1,0:T(4,128)} %sm.1, f32[3,256]{1,0:T(4,128)} %sv.1, f32[128,256]{1,0:T(8,128)} %cur.1, s32[6,16]{1,0:T(8,128)} %part.1, s32[6,1,24]{2,1,0:T(1,128)} %eb.1, ...), custom_call_target="tpu_custom_call" | custom-call | tf_op jit(solution)/shard_map/interface_cg/pallas_call | solution.py:579
  149.3 1.6 %settle.1 = (f32[1,6,24,128]{3,2,1,0:T(8,128)}, f32[1,256,128]{2,1,0:T(8,128)}) custom-call(f32[1,6,24,128]{3,2,1,0:T(8,128)} %get-tuple-element.4.mult, f32[1,256,128]{2,1,0:T(8,128)} %get-tuple-element.5.trace), custom_call_target="tpu_custom_call" | custom-call | tf_op jit(solution)/shard_map/settle/pallas_call | solution.py:590

commit v4 on v3

--- a/solution.py
+++ b/solution.py
@@ -23,6 +23,7 @@
 MESH = pl.DeviceIdType.MESH
 
 PLANE = ((0, 1), (1, 0), (-1, 0), (1, 1), (-1, 1), (2, 0), (2, 1))
+ALONG = (1, -1, 2)
 NEAR = ((0, 1), (1, 0), (-1, 0), (1, 1), (-1, 1))
 FAR = (3, -3)
 COLUMN = tuple((dz, fy) for dz in (4, -3, 3, -2, 2, -1, 1, 0) for fy in (1, 0) if dz or fy)
@@ -39,11 +40,11 @@
 
 def kernel(em, ed, sm, sv, cur, part, eb, flex,
            mult_out, trace_out,
-           geo, ge, cg, sg, xg, fg, ps, pr, pps, ppr, fps, fpr,
+           geo, ge, cg, sg, xg, fg, ps, pr, pps, ppr, fps, fpr, cps, cpr, yps, ypr,
            wa0, wa1, wa2, wa3, wb0, wb1, wb2, wb3, fw, far_s, far_r,
            fv, fhi, flo, fsh, fsl, fssh, fssl, rem, kh, kl, cb, xb, pt, pk, ptb, pb, est, ebc,
            sgn, own, base, tx, tr, tp, trp, tsp, vr, vs, vp, vx,
-           fsem, fsend, frecv, esend, erecv, gsend, grecv, dsend, drecv, psend, precv,
+           fsem, fsend, frecv, esend, erecv, gsend, grecv, dsend, drecv, psend, precv, ysend, yrecv,
            nsend, nrecv, zsend, zrecv, asend, arecv):
     seg = lax.axis_index("seg")
     sub = lax.axis_index("sub")
@@ -85,32 +86,49 @@
         copy.start()
         flex_copies.append(copy)
     barrier = pltpu.get_barrier_semaphore()
-    peers = [plane_dev(dx, fy, 0) for dx, fy in PLANE] + [sibling]
+    peers = [plane_dev(dx, fy, 0) for dx, fy in PLANE] + [sibling, plane_dev(0, 1, 1)]
     peers += [column_dev(dz, fy) for dz, fy in COLUMN]
     for peer in peers:
         pl.semaphore_signal(barrier, inc=1, device_id=peer, device_id_type=MESH)
-    geo[q, 0:3, :] = sm[...]
-    geo[q, 3:6, :] = sv[...]
-    geo[q, 6:8, :] = jnp.zeros((2, ROWS), f32)
+    geo[x, 0:3, :] = sm[...]
+    geo[x, 3:6, :] = sv[...]
+    geo[x, 6:8, :] = jnp.zeros((2, ROWS), f32)
+    my_set = ylo * 2 + c
     for comp in range(3):
-        ge[c, comp:comp + 1, :] = em[comp]
-        ge[c, 3 + comp:4 + comp, :] = ed[comp]
-    ge[c, 6:8, :] = jnp.zeros((2, ROWS), f32)
+        ge[my_set, comp:comp + 1, :] = em[comp]
+        ge[my_set, 3 + comp:4 + comp, :] = ed[comp]
+    ge[my_set, 6:8, :] = jnp.zeros((2, ROWS), f32)
     turned = cur[...].T
     left = low_lanes(LANES)
-    cg[0, q] = jnp.where(left, turned[:LANES], swap(turned[LANES:]))
-    cg[1, q] = jnp.where(left, swap(turned[:LANES]), turned[LANES:])
+    cg[0, x] = jnp.where(left, turned[:LANES], swap(turned[LANES:]))
+    cg[1, x] = jnp.where(left, swap(turned[:LANES]), turned[LANES:])
     pl.semaphore_wait(barrier, len(peers))
 
-    edge_copy = remote(ge.at[c], ge.at[c], esend, erecv, sibling)
-    edge_copy.start()
-    pending.append(edge_copy)
+    edge_copies = []
+    for k, (fy, fc) in enumerate(((0, 1), (1, 0), (1, 1))):
+        copy = remote(ge.at[my_set], ge.at[my_set], esend.at[k], erecv.at[k], plane_dev(0, fy, fc))
+        copy.start()
+        edge_copies.append(copy)
     geo_copies = []
-    for k, (dx, fy) in enumerate(PLANE):
-        copy = remote(geo.at[q], geo.at[q], gsend.at[k], grecv.at[k], plane_dev(dx, fy, 0))
+    for k, dx in enumerate(ALONG):
+        copy = remote(geo.at[x], geo.at[x], gsend.at[k], grecv.at[k], plane_dev(dx, 0, 0))
         copy.start()
         geo_copies.append(copy)
-    pending.extend(geo_copies)
+    pending.extend(edge_copies + geo_copies)
+
+    def along_start(h):
+        for k, dx in enumerate(ALONG):
+            copy = remote(cg.at[h, x], cg.at[h, x], dsend.at[h, k], drecv.at[h, k], plane_dev(dx, 0, 0))
+            copy.start()
+            pending.append(copy)
+
+    def along_wait(h, each):
+        each(x)
+        for k, dx in enumerate(ALONG):
+            origin = (x - dx + 4) % 4
+            here = cg.at[h, origin]
+            remote(here, here, dsend.at[h, k], drecv.at[h, k], sibling).wait_recv()
+            each(origin)
 
     def gather_start(buf, g):
         mine = buf.at[q]
@@ -127,8 +145,8 @@
             remote(here, here, dsend.at[g, k], drecv.at[g, k], sibling).wait_recv()
             each(origin)
 
-    gather_start(cg.at[0], 0)
-    gather_start(cg.at[1], 1)
+    along_start(0)
+    along_start(1)
     shared_copies = []
     for chip in range(CHIPS):
         src = flex.at[0, :, pl.ds(pl.multiple_of((chip * 2 + 1 - c) * ROWS, ROWS), ROWS)]
@@ -154,8 +172,9 @@
     ptb[...] = pt[0:PICKS, :].astype(bf16)
     pb[...] = pk[...].T
 
-    edge_copy.wait_recv()
-    for side in range(2):
+    for copy in edge_copies:
+        copy.wait_recv()
+    for side in range(4):
         est[...] = jnp.zeros((LANES, ROWS), f32)
         est[0:8, :] = ge[side]
         columns = est[...].T
@@ -175,7 +194,7 @@
         copy.wait_recv()
 
     def tile(step, carry):
-        side, chip = step // CHIPS, step % CHIPS
+        side, chip = step // 4, step % 4
         for h in range(2):
             row = [geo[chip, pl.ds(comp, 1), h * LANES:(h + 1) * LANES] for comp in range(6)]
             lanes = pl.ds(pl.multiple_of(chip * ROWS + h * LANES, LANES), LANES)
@@ -191,7 +210,7 @@
                 kh[side, rows, lanes] = high
                 kl[side, rows, lanes] = low
         return carry
-    lax.fori_loop(0, 2 * CHIPS, tile, 0)
+    lax.fori_loop(0, 16, tile, 0)
 
     def unpack(value):
         high = value.astype(bf16).astype(f32)
@@ -367,10 +386,30 @@
         return jnp.concatenate([gamma, delta, jnp.zeros((6, LANES), f32)], axis=0)
 
     def chain(h):
-        gather_wait(cg.at[h], h, dense_block(cg.at[h], h))
+        along_wait(h, dense_block(cg.at[h], h))
         yield
-        total, _ = combine(h, dense_dot(kh, kl, h), zeros8)
-        sg[h, q] = jnp.where(left, total[:LANES], total[LANES:])
+
+        def part_of(yy, cc):
+            side = yy * 2 + cc
+            rows = cb[h, 0:4 * ROWS, :]
+            got = dot(kh[side], rows) + dot(kl[side], rows)
+            got = got + swap(got)
+            return jnp.where(left, got[:LANES], got[LANES:])
+        cps[h, 0:LANES, :] = part_of(1 - ylo, 1 - c)
+        cps[h, LANES:, :] = part_of(ylo, 1 - c)
+        copy = remote(cps.at[h], cpr.at[h], psend.at[h], precv.at[h], sibling)
+        copy.start()
+        pending.append(copy)
+        away = part_of(1 - ylo, c)
+        copy.wait_recv()
+        yps[h] = away + cpr[h, 0:LANES, :]
+        copy = remote(yps.at[h], ypr.at[h], ysend.at[h], yrecv.at[h], plane_dev(0, 1, 0))
+        copy.start()
+        pending.append(copy)
+        here = part_of(ylo, c) + cpr[h, LANES:, :]
+        yield
+        copy.wait_recv()
+        sg[h, q] = here + ypr[h]
         gather_start(sg.at[h], 2 + h)
         yield
         gather_wait(sg.at[h], 2 + h, dense_block(sg.at[h], h))
@@ -501,8 +540,10 @@
     lax.fori_loop(0, 2 * CHIPS, split_flex, 0)
     go(0)
     go(0)
+    go(1)
+    go(0)
+    go(1)
     pick_columns(0)
-    go(1)
     go(1)
     pick_columns(1)
     for which in (0, 0, 1, 1, 0, 1, 0, 1, 0, 0, 1, 1):
@@ -545,13 +586,14 @@
         return pltpu.VMEM(shape, bf16)
     both = 2 * ITERS
     scratch = [
-        room(CHIPS, 8, ROWS), room(2, 8, ROWS),
-        room(2, CHIPS, LANES, LANES),
+        room(4, 8, ROWS), room(4, 8, ROWS),
+        room(2, 4, LANES, LANES),
         room(2, CHIPS, LANES, LANES),
         room(both, CHIPS, MSG, LANES),
         room(2, CHIPS, 8, LANES),
         room(18, LANES + 8, LANES), room(18, LANES + 8, LANES),
         room(12, MSG, LANES), room(12, MSG, LANES), room(2, 8, LANES), room(2, 8, LANES),
+        room(2, 2 * LANES, LANES), room(2, 2 * LANES, LANES), room(2, LANES, LANES), room(2, LANES, LANES),
     ]
     scratch += [room(6, MSG, LANES)] * both
     scratch += [room(2, 16, 8, LANES), room(both, 2, MSG, LANES), room(both, 2, MSG, LANES)]
@@ -559,17 +601,17 @@
         room(2, ROWS, half), short(2, ROWS, half), short(2, ROWS, half),
         short(2, ROWS, DEPTH), short(2, ROWS, DEPTH),
         short(2, PICKS, DEPTH), short(2, PICKS, DEPTH), room(2, ROWS, LANES),
-        short(2, ROWS, half), short(2, ROWS, half),
+        short(4, ROWS, 4 * ROWS), short(4, ROWS, 4 * ROWS),
         short(2, half, LANES), short(2, DEPTH, LANES),
         room(ROWS, ROWS), room(ROWS, ROWS), short(PICKS, ROWS), room(ROWS, ROWS),
-        room(LANES, ROWS), room(2, 6, ROWS, LANES),
+        room(LANES, ROWS), room(4, 6, ROWS, LANES),
         room(BAND, LANES), room(BAND, LANES),
     ]
     scratch += [room(2, ROWS, LANES)] * 4
     scratch += [room(2, BAND, LANES)] * 6
     scratch += [
-        dma((8,)), dma((8,)), dma((8,)), dma, dma, dma((7,)), dma((7,)),
-        dma((14, 7)), dma((14, 7)), dma((20,)), dma((20,)),
+        dma((8,)), dma((8,)), dma((8,)), dma((3,)), dma((3,)), dma((3,)), dma((3,)),
+        dma((14, 7)), dma((14, 7)), dma((20,)), dma((20,)), dma((2,)), dma((2,)),
         dma((8, 5)), dma((8, 5)), dma((8, 2)), dma((8, 2)), dma((2, 15)), dma((2, 15)),
     ]
     outs = (

time: 151 us -> 152 us (level)
  no operation moved by 1% of the time
where the time goes in v4:
time: 152 us
  Pallas kernels  151 us (99%)
    pallas_call x1, Pallas kernels, body(): pl.pallas_call(kernel, out_shape=outs, in_specs=[vmem] * 5 + [smem] * 2 +...  149 us

profile of v4, /device:TPU:1, one launch (start us, length us, event | category | flops | bytes accessed | tf_op | source)
XLA Modules:
  0.0 151.6 jit_solution(14722852880371599827)
XLA Ops:
  0.6 149.3 %interface_cg.1 = (f32[1,6,24,128]{3,2,1,0:T(8,128)}, f32[1,256,128]{2,1,0:T(8,128)}) custom-call(f32[3,1,256]{2,1,0:T(1,128)} %bitcast.2, f32[3,1,256]{2,1,0:T(1,128)} %bitcast.3, f32[3,256]{1,0:T(4,128)} %sm.1, f32[3,256]{1,0:T(4,128)} %sv.1, f32[128,256]{1,0:T(8,128)} %cur.1, s32[6,16]{1,0:T(8,128)} %part.1, s32[6,1,24]{2,1,0:T(1,128)} %eb.1, ...), custom_call_target="tpu_custom_call" | custom-call | tf_op jit(solution)/shard_map/interface_cg/pallas_call | solution.py:621
  149.9 1.6 %settle.1 = (f32[1,6,24,128]{3,2,1,0:T(8,128)}, f32[1,256,128]{2,1,0:T(8,128)}) custom-call(f32[1,6,24,128]{3,2,1,0:T(8,128)} %get-tuple-element.4.mult, f32[1,256,128]{2,1,0:T(8,128)} %get-tuple-element.5.trace), custom_call_target="tpu_custom_call" | custom-call | tf_op jit(solution)/shard_map/settle/pallas_call | solution.py:632

commit v5 on v4

--- a/solution.py
+++ b/solution.py
@@ -546,12 +546,8 @@
     pick_columns(0)
     go(1)
     pick_columns(1)
-    for which in (0, 0, 1, 1, 0, 1, 0, 1, 0, 0, 1, 1):
-        go(which)
-    for _ in range(ITERS - 2):
-        for which in (0, 1, 0, 1, 0, 0, 1, 1):
-            go(which)
-    for which in (0, 1, 0, 1, 0, 0, 0, 1, 1, 0, 1, 1, 0, 0, 1, 1):
+    turn = (0, 0, 1, 1, 0, 0, 1, 1)
+    for which in (0, 0, 1, 1) + turn * (ITERS - 1) + (0, 0, 1, 1, 0, 0, 0, 1, 1, 0, 1, 1, 0, 0, 1, 1):
         go(which)
 
     side = low_lanes(ROWS)

time: 152 us -> 157 us (1.033)
  Pallas kernels: 151 us -> 156 us
    pallas_call x1, Pallas kernels: 149 us -> 154 us  [body(): pl.pallas_call(kernel, out_shape=outs, in_specs=[vmem] * 5 + [smem] * 2 +...]
where the time goes in v5:
time: 157 us
  Pallas kernels  156 us (99%)
    pallas_call x1, Pallas kernels, body(): pl.pallas_call(kernel, out_shape=outs, in_specs=[vmem] * 5 + [smem] * 2 +...  154 us

profile of v5, /device:TPU:1, one launch (start us, length us, event | category | flops | bytes accessed | tf_op | source)
XLA Modules:
  0.0 156.6 jit_solution(14536085910929363709)
XLA Ops:
  0.6 154.3 %interface_cg.1 = (f32[1,6,24,128]{3,2,1,0:T(8,128)}, f32[1,256,128]{2,1,0:T(8,128)}) custom-call(f32[3,1,256]{2,1,0:T(1,128)} %bitcast.2, f32[3,1,256]{2,1,0:T(1,128)} %bitcast.3, f32[3,256]{1,0:T(4,128)} %sm.1, f32[3,256]{1,0:T(4,128)} %sv.1, f32[128,256]{1,0:T(8,128)} %cur.1, s32[6,16]{1,0:T(8,128)} %part.1, s32[6,1,24]{2,1,0:T(1,128)} %eb.1, ...), custom_call_target="tpu_custom_call" | custom-call | tf_op jit(solution)/shard_map/interface_cg/pallas_call | solution.py:617
  154.9 1.6 %settle.1 = (f32[1,6,24,128]{3,2,1,0:T(8,128)}, f32[1,256,128]{2,1,0:T(8,128)}) custom-call(f32[1,6,24,128]{3,2,1,0:T(8,128)} %get-tuple-element.4.mult, f32[1,256,128]{2,1,0:T(8,128)} %get-tuple-element.5.trace), custom_call_target="tpu_custom_call" | custom-call | tf_op jit(solution)/shard_map/settle/pallas_call | solution.py:628

commit v6 on v3

--- a/solution.py
+++ b/solution.py
@@ -22,7 +22,7 @@
 bf16 = jnp.bfloat16
 MESH = pl.DeviceIdType.MESH
 
-PLANE = ((0, 1), (1, 0), (-1, 0), (1, 1), (-1, 1), (2, 0), (2, 1))
+PLANE = ((2, 1), (1, 1), (-1, 1), (2, 0), (1, 0), (-1, 0), (0, 1))
 NEAR = ((0, 1), (1, 0), (-1, 0), (1, 1), (-1, 1))
 FAR = (3, -3)
 COLUMN = tuple((dz, fy) for dz in (4, -3, 3, -2, 2, -1, 1, 0) for fy in (1, 0) if dz or fy)

time: 151 us -> 148 us (0.980)
  Pallas kernels: 150 us -> 147 us
    pallas_call x1, Pallas kernels: 149 us -> 146 us  [body(): pl.pallas_call(kernel, out_shape=outs, in_specs=[vmem] * 5 + [smem] * 2 +...]
where the time goes in v6:
time: 148 us
  Pallas kernels  147 us (99%)
    pallas_call x1, Pallas kernels, body(): pl.pallas_call(kernel, out_shape=outs, in_specs=[vmem] * 5 + [smem] * 2 +...  146 us

profile of v6, /device:TPU:1, one launch (start us, length us, event | category | flops | bytes accessed | tf_op | source)
XLA Modules:
  0.0 148.1 jit_solution(9489071102690747176)
XLA Ops:
  0.6 145.9 %interface_cg.1 = (f32[1,6,24,128]{3,2,1,0:T(8,128)}, f32[1,256,128]{2,1,0:T(8,128)}) custom-call(f32[3,1,256]{2,1,0:T(1,128)} %bitcast.2, f32[3,1,256]{2,1,0:T(1,128)} %bitcast.3, f32[3,256]{1,0:T(4,128)} %sm.1, f32[3,256]{1,0:T(4,128)} %sv.1, f32[128,256]{1,0:T(8,128)} %cur.1, s32[6,16]{1,0:T(8,128)} %part.1, s32[6,1,24]{2,1,0:T(1,128)} %eb.1, ...), custom_call_target="tpu_custom_call" | custom-call | tf_op jit(solution)/shard_map/interface_cg/pallas_call | solution.py:579
  146.5 1.6 %settle.1 = (f32[1,6,24,128]{3,2,1,0:T(8,128)}, f32[1,256,128]{2,1,0:T(8,128)}) custom-call(f32[1,6,24,128]{3,2,1,0:T(8,128)} %get-tuple-element.4.mult, f32[1,256,128]{2,1,0:T(8,128)} %get-tuple-element.5.trace), custom_call_target="tpu_custom_call" | custom-call | tf_op jit(solution)/shard_map/settle/pallas_call | solution.py:590

commit v7 on v6

--- a/solution.py
+++ b/solution.py
@@ -23,7 +23,7 @@
 MESH = pl.DeviceIdType.MESH
 
 PLANE = ((2, 1), (1, 1), (-1, 1), (2, 0), (1, 0), (-1, 0), (0, 1))
-NEAR = ((0, 1), (1, 0), (-1, 0), (1, 1), (-1, 1))
+NEAR = ((1, 1), (-1, 1), (0, 1), (1, 0), (-1, 0))
 FAR = (3, -3)
 COLUMN = tuple((dz, fy) for dz in (4, -3, 3, -2, 2, -1, 1, 0) for fy in (1, 0) if dz or fy)
 

time: 148 us -> 149 us (level)
  Pallas kernels: 147 us -> 149 us
where the time goes in v7:
time: 149 us
  Pallas kernels  149 us (100%)
    pallas_call x1, Pallas kernels, body(): pl.pallas_call(kernel, out_shape=outs, in_specs=[vmem] * 5 + [smem] * 2 +...  147 us

profile of v7, /device:TPU:1, one launch (start us, length us, event | category | flops | bytes accessed | tf_op | source)
XLA Modules:
  0.0 149.3 jit_solution(11575186473511987070)
XLA Ops:
  0.6 147.0 %interface_cg.1 = (f32[1,6,24,128]{3,2,1,0:T(8,128)}, f32[1,256,128]{2,1,0:T(8,128)}) custom-call(f32[3,1,256]{2,1,0:T(1,128)} %bitcast.2, f32[3,1,256]{2,1,0:T(1,128)} %bitcast.3, f32[3,256]{1,0:T(4,128)} %sm.1, f32[3,256]{1,0:T(4,128)} %sv.1, f32[128,256]{1,0:T(8,128)} %cur.1, s32[6,16]{1,0:T(8,128)} %part.1, s32[6,1,24]{2,1,0:T(1,128)} %eb.1, ...), custom_call_target="tpu_custom_call" | custom-call | tf_op jit(solution)/shard_map/interface_cg/pallas_call | solution.py:579
  147.6 1.6 %settle.1 = (f32[1,6,24,128]{3,2,1,0:T(8,128)}, f32[1,256,128]{2,1,0:T(8,128)}) custom-call(f32[1,6,24,128]{3,2,1,0:T(8,128)} %get-tuple-element.4.mult, f32[1,256,128]{2,1,0:T(8,128)} %get-tuple-element.5.trace), custom_call_target="tpu_custom_call" | custom-call | tf_op jit(solution)/shard_map/settle/pallas_call | solution.py:590
